TPU v7x, 128 devices: a whole 4x4x4 slice. The times are simulated.
128 devices in a mesh: section: 8 (over x, y_lo), tile: 16 (over z, y_hi, core).
Axes of the slice: x: 4, y: 4 (y_hi: 2, y_lo: 2; y = y_hi * 2 + y_lo), z: 4, core: 2. Of those that a mesh axis runs over, the one named last changes fastest.
Arguments:
- latents: bfloat16 [8, 6144, 1536], P('section', 'tile'), may hold values from -6 to 6
- query_key_value_weight: bfloat16 [8, 1536, 4608], P('section'), may hold values from -0.15625 to 0.15625
- output_weight_stack: bfloat16 [8, 1536, 1536], P('section'), may hold values from -0.15625 to 0.15625
- layer_norm_gains: float32 [8, 1536], P('section'), may hold values from 0.5 to 2
- attended_tile_lists: int32 [16, 3], P('tile'), may hold values from 0 to 15, as said below
- neighbour_tile_count: int32 [16], P('tile'), may hold values from 1 to 3
Outputs:
- advanced: bfloat16 [8, 6144, 1536], P('section', 'tile')
Inputs may be any that keep to these rules, and one draw needn't show every extreme that they name: `attended_tile_lists`: the tiles listed for tile t lie among the tiles of the index of tile that holds t and of its two neighbours on that axis; the first entry is t itself and the first neighbour_tile_count[t] entries are distinct.
All inputs are finite; a program needn't handle non-finite values.
Results may differ from a plain program's by a relative error of at most 0.02.
Values may be sent and summed in bfloat16 or wider, within the bound.
No kernel may reach another device: no remote copies, remote signals or barrier semaphores. Data moves between devices by JAX's collectives and lax.ppermute only.
A program may use at most 128 MiB of HBM per device.

v0:
```python
import jax
import jax.numpy as jnp
from jax import lax
from jax.sharding import PartitionSpec as P

HEADS = 12
HD = 128
D = 1536
TS = 384
NBR = 3
HOPS = 2


def padded(cells, sides, width):
    for axis, dim in sides:
        count = lax.axis_size(axis)
        ends = count - 1
        head = lax.slice_in_dim(cells, 0, width, axis=dim)
        tail = lax.slice_in_dim(cells, cells.shape[dim] - width, cells.shape[dim], axis=dim)
        cells = jnp.concatenate(
            [
                lax.ppermute(tail, axis, [(i, (i + 1) % count) for i in range(ends)]),
                cells,
                lax.ppermute(head, axis, [((i + 1) % count, i) for i in range(ends)]),
            ],
            axis=dim,
        )
    return cells


def from_behind(block, axis, distance):
    devices = range(lax.axis_size(axis))
    route = [((i - distance) % len(devices), i) for i in devices]
    return lax.ppermute(block, axis, route)


def normalize(hidden_activations, norm_gain_vector):
    widened = hidden_activations.astype(jnp.float32)
    square = jnp.mean(widened * widened, axis=-1, keepdims=True)
    return (widened * lax.rsqrt(square + 1e-06) * norm_gain_vector).astype(jnp.bfloat16)


def softmax_weights(scores, allowed):
    masked = jnp.where(allowed, scores, -jnp.inf)
    highest = jnp.max(masked, axis=-1, keepdims=True)
    raised = jnp.exp(masked - highest)
    return (raised / jnp.sum(raised, axis=-1, keepdims=True)).astype(jnp.bfloat16)


def diffusion_layer_step(
    hidden_activations,
    norm_gain_vector,
    query_key_value_layer,
    output_projection_layer,
    attended_tile_lists,
    neighbour_tile_count,
):
    tiles_here = attended_tile_lists.shape[0]
    rows_here = hidden_activations.shape[0]
    normed = normalize(hidden_activations, norm_gain_vector)
    projected = jnp.dot(normed, query_key_value_layer, preferred_element_type=jnp.float32).astype(
        jnp.bfloat16
    )
    query_flat = projected[:, :D]
    paired = padded(projected[:, D:], (("tile", 0),), rows_here)
    query = query_flat.reshape(tiles_here, TS, HEADS, HD)
    near_tiles = 3 * tiles_here
    key_tiles = paired[:, :D].reshape(near_tiles, TS, HEADS, HD)
    value_tiles = paired[:, D:].reshape(near_tiles, TS, HEADS, HD)
    first_tile = (lax.axis_index("tile") - 1) * tiles_here
    relative = attended_tile_lists - first_tile
    scale = HD ** (-0.5)
    key_rows = key_tiles[relative].reshape(tiles_here, NBR * TS, HEADS, HD)
    value_rows = value_tiles[relative].reshape(tiles_here, NBR * TS, HEADS, HD)
    scores = (
        jnp.einsum("tqhd,tkhd->thqk", query, key_rows, preferred_element_type=jnp.float32) * scale
    )
    slot_index = jnp.arange(NBR * TS, dtype=jnp.int32) // TS
    allowed = (slot_index[None, :] < neighbour_tile_count[:, None])[:, None, None, :]
    probs = softmax_weights(scores, allowed)
    mixed = jnp.einsum("thqk,tkhd->tqhd", probs, value_rows, preferred_element_type=jnp.float32)
    mixed = mixed.astype(jnp.bfloat16).reshape(rows_here, D)
    update = jnp.dot(mixed, output_projection_layer, preferred_element_type=jnp.float32)
    return (hidden_activations.astype(jnp.float32) + update).astype(jnp.bfloat16)


def on_device(
    latents,
    query_key_value_weight,
    output_weight_stack,
    layer_norm_gains,
    attended_tile_lists,
    neighbour_tile_count,
):
    hidden_activations = latents[0]
    for passed in range(HOPS):
        hidden_activations = diffusion_layer_step(
            hidden_activations,
            layer_norm_gains[0],
            query_key_value_weight[0],
            output_weight_stack[0],
            attended_tile_lists,
            neighbour_tile_count,
        )
        hidden_activations = from_behind(hidden_activations, "section", 1)
    return hidden_activations[None]


def solution(mesh):
    return jax.shard_map(
        on_device,
        mesh=mesh,
        in_specs=(
            P("section", "tile", None),
            P("section", None, None),
            P("section", None, None),
            P("section", None),
            P("tile", None),
            P("tile"),
        ),
        out_specs=P("section", "tile", None),
        check_vma=False,
    )
```

profile of v0, /device:TPU:33, one launch (start us, length us, event | category | flops | bytes accessed | tf_op | source)
XLA Modules:
  0.0 376.3 jit_solution(5070132530550048106)
XLA Ops:
  2.3 11.3 %fusion.10 = bf16[384,4608]{1,0:T(8,128)(2,1)S(1)} fusion(bf16[1,1536,4608]{2,1,0:T(8,128)(2,1)} %param.7, bf16[1,384,1536]{2,1,0:T(8,128)(2,1)} %param.6, f32[1536]{0:T(1024)S(1)} %reduce.8, f32[384]{0:T(512)S(1)} %add_rsqrt_fusion.1), kind=kOutput, calls=%fused_computation.22 | convolution fusion | flops 5439946752 | bytes 18882048 | tf_op jit(solution)/shard_map/dot_general | solution.py:61
  13.9 5.4 %collective-permute-start = (bf16[384,3072]{1,0:T(8,128)(2,1)S(1)}, bf16[384,3072]{1,0:T(8,128)(2,1)}, u32[]{:S(2)}, u32[]{:S(2)}) collective-permute-start(bf16[384,3072]{1,0:T(8,128)(2,1)S(1)} %slice.40), channel_id=1, source_target_pairs={{0,1},{1,2},{2,3},{3,4},{4,5},{5,6},{6,7},{7,8},{8,9},{9,10},{10,1... | collective-permute-start | bytes 7077896 | tf_op jit(solution)/shard_map/ppermute | solution.py:22
  23.8 43.1 %collective-permute-done = bf16[384,3072]{1,0:T(8,128)(2,1)} collective-permute-done((bf16[384,3072]{1,0:T(8,128)(2,1)S(1)}, bf16[384,3072]{1,0:T(8,128)(2,1)}, u32[]{:S(2)}, u32[]{:S(2)}) %collective-permute-start) | collective-permute-done | bytes 2359328 | tf_op jit(solution)/shard_map/ppermute | solution.py:22
  66.9 5.5 %collective-permute-done.1 = bf16[384,3072]{1,0:T(8,128)(2,1)} collective-permute-done((bf16[384,3072]{1,0:T(8,128)(2,1)S(1)}, bf16[384,3072]{1,0:T(8,128)(2,1)}, u32[]{:S(2)}, u32[]{:S(2)}) %collective-permute-start.1) | collective-permute-done | bytes 2359328 | tf_op jit(solution)/shard_map/ppermute | solution.py:24
  78.1 7.3 %reshape.146 = bf16[3,384,12,128]{3,2,1,0:T(8,128)(2,1)} reshape(bf16[1152,1536]{1,0:T(8,128)(2,1)} %get-tuple-element.8) | data formatting | bytes 7077888 | tf_op jit(solution)/shard_map/reshape | solution.py:68
  85.4 5.8 %gather_fusion.1 = bf16[3,384,12,128]{3,2,1,0:T(8,128)(2,1)} fusion(bf16[3,384,12,128]{3,2,1,0:T(8,128)(2,1)} %reshape.146, s32[1024]{0:T(1024)S(1)} %pad_clamp_fusion), kind=kCustom, calls=%fused_computation.1 | custom fusion | bytes 7077900 | tf_op jit(solution)/shard_map/gather | solution.py:73
  91.3 13.3 %multiply_select_fusion.1 = f32[12,384,1152]{2,1,0:T(8,128)} fusion(bf16[384,12,128]{0,2,1:T(8,128)(2,1)} %bitcast.66, pred[1152]{0:T(1024)(128)(4,1)S(1)} %fusion.55, bf16[1152,12,128]{2,1,0:T(8,128)(2,1)} %bitcast.65), kind=kOutput, calls=%fused_computation.11 | convolution fusion | flops 1369571328 | bytes 25953408 | tf_op jit(solution)/shard_map/tqhd,tkhd->thqk/dot_general | solution.py:76
  104.6 17.9 %exponential_reduce_fusion.1 = f32[12,384]{1,0:T(8,128)} fusion(f32[12,384,1152]{2,1,0:T(8,128)} %multiply_select_fusion.1), kind=kOutput, calls=%fused_computation.13 | output fusion | flops 10617983 | bytes 21252096 | tf_op jit(solution)/shard_map/sub | solution.py:46
  122.5 4.4 %reshape.143 = bf16[3,384,12,128]{3,2,1,0:T(8,128)(2,1)} reshape(bf16[1152,1536]{1,0:T(8,128)(2,1)S(1)} %get-tuple-element.7) | data formatting | bytes 7077888 | tf_op jit(solution)/shard_map/reshape | solution.py:69
  126.9 5.8 %gather_fusion = bf16[3,384,12,128]{3,2,1,0:T(8,128)(2,1)} fusion(bf16[3,384,12,128]{3,2,1,0:T(8,128)(2,1)} %reshape.143, s32[1024]{0:T(1024)S(1)} %pad_clamp_fusion), kind=kCustom, calls=%fused_computation | custom fusion | bytes 7077900 | tf_op jit(solution)/shard_map/gather | solution.py:74
  132.7 23.3 %fusion.45 = bf16[12,128,384]{2,1,0:T(8,128)(2,1)S(1)} fusion(f32[12,384]{1,0:T(8,128)S(1)} %copy-done.4, bf16[1152,12,128]{2,1,0:T(8,128)(2,1)} %bitcast.69, f32[12,384,1152]{2,1,0:T(8,128)} %multiply_select_fusion.1), kind=kOutput, calls=%fused_computation.48 | convolution fusion | flops 1375475328 | bytes 25970688 | tf_op jit(solution)/shard_map/thqk,tkhd->tqhd/dot_general | solution.py:81
  161.8 27.4 %collective-permute-done.2 = bf16[384,1536]{1,0:T(8,128)(2,1)S(1)} collective-permute-done((bf16[384,1536]{1,0:T(8,128)(2,1)S(1)}, bf16[384,1536]{1,0:T(8,128)(2,1)S(1)}, u32[]{:S(2)}, u32[]{:S(2)}) %collective-permute-start.2) | collective-permute-done | bytes 1179680 | tf_op jit(solution)/shard_map/ppermute | solution.py:34
  189.5 11.2 %fusion.13 = bf16[384,4608]{1,0:T(8,128)(2,1)S(1)} fusion(bf16[1,1536,4608]{2,1,0:T(8,128)(2,1)} %param.7, bf16[384,1536]{1,0:T(8,128)(2,1)S(1)} %collective-permute-done.2, f32[1536]{0:T(1024)S(1)} %reduce.8, f32[384]{0:T(512)S(1)} %add_rsqrt_fusion), kind=kOutput, calls=%fused_computation.23 | convolution fusion | flops 5439946752 | bytes 18882048 | tf_op jit(solution)/shard_map/dot_general | solution.py:61
  207.0 41.1 %collective-permute-done.3 = bf16[384,3072]{1,0:T(8,128)(2,1)} collective-permute-done((bf16[384,3072]{1,0:T(8,128)(2,1)S(1)}, bf16[384,3072]{1,0:T(8,128)(2,1)}, u32[]{:S(2)}, u32[]{:S(2)}) %collective-permute-start.3) | collective-permute-done | bytes 2359328 | tf_op jit(solution)/shard_map/ppermute | solution.py:22
  248.1 10.5 %collective-permute-done.4 = bf16[384,3072]{1,0:T(8,128)(2,1)} collective-permute-done((bf16[384,3072]{1,0:T(8,128)(2,1)S(1)}, bf16[384,3072]{1,0:T(8,128)(2,1)}, u32[]{:S(2)}, u32[]{:S(2)}) %collective-permute-start.4) | collective-permute-done | bytes 2359328 | tf_op jit(solution)/shard_map/ppermute | solution.py:24
  264.3 7.3 %reshape.152 = bf16[3,384,12,128]{3,2,1,0:T(8,128)(2,1)} reshape(bf16[1152,1536]{1,0:T(8,128)(2,1)} %get-tuple-element.6) | data formatting | bytes 7077888 | tf_op jit(solution)/shard_map/reshape | solution.py:68
  271.7 5.8 %gather_fusion.3 = bf16[3,384,12,128]{3,2,1,0:T(8,128)(2,1)} fusion(bf16[3,384,12,128]{3,2,1,0:T(8,128)(2,1)} %reshape.152, s32[1024]{0:T(1024)S(1)} %pad_clamp_fusion), kind=kCustom, calls=%fused_computation.3 | custom fusion | bytes 7077900 | tf_op jit(solution)/shard_map/gather | solution.py:73
  277.5 13.3 %multiply_select_fusion = f32[12,384,1152]{2,1,0:T(8,128)} fusion(bf16[384,12,128]{0,2,1:T(8,128)(2,1)} %bitcast.67, pred[1152]{0:T(1024)(128)(4,1)S(1)} %fusion.55, bf16[1152,12,128]{2,1,0:T(8,128)(2,1)} %bitcast.64), kind=kOutput, calls=%fused_computation.9 | convolution fusion | flops 1369571328 | bytes 25953408 | tf_op jit(solution)/shard_map/tqhd,tkhd->thqk/dot_general | solution.py:76
  290.8 17.9 %exponential_reduce_fusion = f32[12,384]{1,0:T(8,128)} fusion(f32[12,384,1152]{2,1,0:T(8,128)} %multiply_select_fusion), kind=kOutput, calls=%fused_computation.12 | output fusion | flops 10617983 | bytes 21252096 | tf_op jit(solution)/shard_map/sub | solution.py:46
  308.8 4.4 %reshape.149 = bf16[3,384,12,128]{3,2,1,0:T(8,128)(2,1)} reshape(bf16[1152,1536]{1,0:T(8,128)(2,1)S(1)} %get-tuple-element.5) | data formatting | bytes 7077888 | tf_op jit(solution)/shard_map/reshape | solution.py:69
  313.1 5.8 %gather_fusion.2 = bf16[3,384,12,128]{3,2,1,0:T(8,128)(2,1)} fusion(bf16[3,384,12,128]{3,2,1,0:T(8,128)(2,1)} %reshape.149, s32[1024]{0:T(1024)S(1)} %pad_clamp_fusion), kind=kCustom, calls=%fused_computation.2 | custom fusion | bytes 7077900 | tf_op jit(solution)/shard_map/gather | solution.py:74
  319.0 23.0 %fusion.42 = bf16[12,128,384]{2,1,0:T(8,128)(2,1)S(1)} fusion(f32[12,384]{1,0:T(8,128)S(1)} %copy-done.3, bf16[1152,12,128]{2,1,0:T(8,128)(2,1)} %bitcast.68, f32[12,384,1152]{2,1,0:T(8,128)} %multiply_select_fusion), kind=kOutput, calls=%fused_computation.47 | convolution fusion | flops 1375475328 | bytes 25970688 | tf_op jit(solution)/shard_map/thqk,tkhd->tqhd/dot_general | solution.py:81
  342.0 4.4 %fusion.33 = bf16[384,1536]{1,0:T(8,128)(2,1)S(1)} fusion(bf16[384,1536]{0,1:T(8,128)(2,1)S(1)} %bitcast.70, bf16[1,1536,1536]{2,1,0:T(8,128)(2,1)} %param.8, bf16[384,1536]{1,0:T(8,128)(2,1)S(1)} %copy-done.2), kind=kOutput, calls=%fused_computation.40 | convolution fusion | flops 1813708800 | bytes 8257536 | tf_op jit(solution)/shard_map/dot_general | solution.py:83
  346.4 28.6 %collective-permute-done.5 = bf16[384,1536]{1,0:T(8,128)(2,1)S(1)} collective-permute-done((bf16[384,1536]{1,0:T(8,128)(2,1)S(1)}, bf16[384,1536]{1,0:T(8,128)(2,1)S(1)}, u32[]{:S(2)}, u32[]{:S(2)}) %collective-permute-start.5) | collective-permute-done | bytes 1179680 | tf_op jit(solution)/shard_map/ppermute | solution.py:34
  (37 shorter events, 31.2 us)
Async XLA Ops:
  13.7 10.1 %copy-start.5 = (s32[1,3]{1,0:T(1,128)S(1)}, s32[1,3]{1,0:T(1,128)}, u32[]{:S(2)}) copy-start(s32[1,3]{1,0:T(1,128)} %param.10) | copy-start | bytes 40
  13.9 52.9 %collective-permute-start = (bf16[384,3072]{1,0:T(8,128)(2,1)S(1)}, bf16[384,3072]{1,0:T(8,128)(2,1)}, u32[]{:S(2)}, u32[]{:S(2)}) collective-permute-start(bf16[384,3072]{1,0:T(8,128)(2,1)S(1)} %slice.40), channel_id=1, source_target_pairs={{0,1},{1,2},{2,3},{3,4},{4,5},{5,6},{6,7},{7,8},{8,9},{9,10},{10,1... | collective-permute-start | bytes 7077896 | tf_op jit(solution)/shard_map/ppermute | solution.py:22
  19.3 53.0 %collective-permute-start.1 = (bf16[384,3072]{1,0:T(8,128)(2,1)S(1)}, bf16[384,3072]{1,0:T(8,128)(2,1)}, u32[]{:S(2)}, u32[]{:S(2)}) collective-permute-start(bf16[384,3072]{1,0:T(8,128)(2,1)S(1)} %slice.40), channel_id=1, source_target_pairs={{1,0},{2,1},{3,2},{4,3},{5,4},{6,5},{7,6},{8,7},{9,8},{10,9},{11,1... | collective-permute-start | bytes 7077896 | tf_op jit(solution)/shard_map/ppermute | solution.py:24
  126.9 5.8 %copy-start.4 = (f32[12,384]{1,0:T(8,128)S(1)}, f32[12,384]{1,0:T(8,128)}, u32[]{:S(2)}) copy-start(f32[12,384]{1,0:T(8,128)} %exponential_reduce_fusion.1) | copy-start | bytes 55300
  132.7 23.3 %copy-start = (bf16[1,384,1536]{2,1,0:T(8,128)(2,1)S(1)}, bf16[1,384,1536]{2,1,0:T(8,128)(2,1)}, u32[]{:S(2)}) copy-start(bf16[1,384,1536]{2,1,0:T(8,128)(2,1)} %param.6) | copy-start | bytes 3538948
  160.4 28.8 %collective-permute-start.2 = (bf16[384,1536]{1,0:T(8,128)(2,1)S(1)}, bf16[384,1536]{1,0:T(8,128)(2,1)S(1)}, u32[]{:S(2)}, u32[]{:S(2)}) collective-permute-start(bf16[384,1536]{1,0:T(8,128)(2,1)S(1)} %fusion.30), channel_id=1, source_target_pairs={{112,0},{0,16},{16,32},{32,48},{48,64},{64,80},{80,96},{96,112},{1... | collective-permute-start | bytes 3538952 | tf_op jit(solution)/shard_map/ppermute | solution.py:34
  189.2 11.5 %copy-start.1 = (bf16[384,1536]{1,0:T(8,128)(2,1)}, bf16[384,1536]{1,0:T(8,128)(2,1)S(1)}, u32[]{:S(2)}) copy-start(bf16[384,1536]{1,0:T(8,128)(2,1)S(1)} %collective-permute-done.2) | copy-start | bytes 3538948
  201.0 47.1 %collective-permute-start.3 = (bf16[384,3072]{1,0:T(8,128)(2,1)S(1)}, bf16[384,3072]{1,0:T(8,128)(2,1)}, u32[]{:S(2)}, u32[]{:S(2)}) collective-permute-start(bf16[384,3072]{1,0:T(8,128)(2,1)S(1)} %slice.44), channel_id=1, source_target_pairs={{0,1},{1,2},{2,3},{3,4},{4,5},{5,6},{6,7},{7,8},{8,9},{9,10},{10,1... | collective-permute-start | bytes 7077896 | tf_op jit(solution)/shard_map/ppermute | solution.py:22
  202.9 55.7 %collective-permute-start.4 = (bf16[384,3072]{1,0:T(8,128)(2,1)S(1)}, bf16[384,3072]{1,0:T(8,128)(2,1)}, u32[]{:S(2)}, u32[]{:S(2)}) collective-permute-start(bf16[384,3072]{1,0:T(8,128)(2,1)S(1)} %slice.44), channel_id=1, source_target_pairs={{1,0},{2,1},{3,2},{4,3},{5,4},{6,5},{7,6},{8,7},{9,8},{10,9},{11,1... | collective-permute-start | bytes 7077896 | tf_op jit(solution)/shard_map/ppermute | solution.py:24
  313.1 5.8 %copy-start.3 = (f32[12,384]{1,0:T(8,128)S(1)}, f32[12,384]{1,0:T(8,128)}, u32[]{:S(2)}) copy-start(f32[12,384]{1,0:T(8,128)} %exponential_reduce_fusion) | copy-start | bytes 55300
  319.0 23.0 %copy-start.2 = (bf16[384,1536]{1,0:T(8,128)(2,1)S(1)}, bf16[384,1536]{1,0:T(8,128)(2,1)}, u32[]{:S(2)}) copy-start(bf16[384,1536]{1,0:T(8,128)(2,1)} %copy-done.1) | copy-start | bytes 3538948
  346.4 28.7 %collective-permute-start.5 = (bf16[384,1536]{1,0:T(8,128)(2,1)S(1)}, bf16[384,1536]{1,0:T(8,128)(2,1)S(1)}, u32[]{:S(2)}, u32[]{:S(2)}) collective-permute-start(bf16[384,1536]{1,0:T(8,128)(2,1)S(1)} %fusion.33), channel_id=1, source_target_pairs={{112,0},{0,16},{16,32},{32,48},{48,64},{64,80},{80,96},{96,112},{1... | collective-permute-start | bytes 3538952 | tf_op jit(solution)/shard_map/ppermute | solution.py:34
where the time goes:
time: 380 us; the launch traced here: 376 us
  waiting for transfers between devices  156 us (41%)
  matrix products  104 us (27%)
  local copies, waits for them, and re-layouts  56.1 us (15%)
  other arithmetic  45.4 us (12%)
  starting transfers between devices  13.4 us (4%)
    ppermute x2, waiting for transfers between devices, padded(): lax.ppermute(tail, axis, [(i, (i + 1) % count) for i in range(ends)])  84.2 us
    ppermute x2, waiting for transfers between devices, from_behind(): return lax.ppermute(block, axis, route)  56 us
    dot_general x2, matrix products, diffusion_layer_step(): jnp.einsum('thqk,tkhd->tqhd', probs, value_rows, preferred_element_type=j...  46.3 us
    sub x2, other arithmetic, softmax_weights(): raised = jnp.exp(masked - highest)  35.9 us
    dot_general x2, matrix products, diffusion_layer_step(): jnp.einsum('tqhd,tkhd->thqk', query, key_rows, preferred_element_type=jnp...  26.7 us
    dot_general x2, matrix products, diffusion_layer_step(): jnp.dot(normed, query_key_value_layer, preferred_element_type=jnp.float32)  22.5 us
    ppermute x2, waiting for transfers between devices, padded(): lax.ppermute(head, axis, [((i + 1) % count, i) for i in range(ends)])  16 us
    reshape x2, local copies, waits for them, and re-layouts, diffusion_layer_step(): key_tiles = paired[:, :D].reshape(near_tiles, TS, HEADS, HD)  14.7 us
  transfers between devices with their start and end apart: 6, of which 6 were waited for; matrix products, arithmetic and copies ran while one was open for 1% of the time, Pallas kernels for 0%

commit v1 on v0

v1 whole, which is shorter than its diff:
```python
import functools
import math

import jax
import jax.numpy as jnp
from jax import lax
from jax.experimental import pallas as pl
from jax.experimental.pallas import tpu as pltpu
from jax.sharding import PartitionSpec as P

HEADS = 12
HD = 128
D = 1536
TS = 384
N_TILE = 16
N_SECTION = 8
PAIR = 2 * HD
PAIRS = HEADS // 2
SCALE = HD ** (-0.5) * math.log2(math.e)
OFF = -1e30
BOTH = ("section", "tile")


def normalize(hidden, gain):
    widened = hidden.astype(jnp.float32)
    square = jnp.mean(widened * widened, axis=-1, keepdims=True)
    return (widened * lax.rsqrt(square + 1e-06) * gain).astype(jnp.bfloat16)


def dot(a, b):
    return jnp.dot(a, b, preferred_element_type=jnp.float32)


def dot_t(a, b):
    return lax.dot_general(a, b, (((1,), (1,)), ((), ())), preferred_element_type=jnp.float32)


def near_kernel(flag_ref, own_ref, near_ref, gain_ref, wq_ref, wk_ref, wv_ref, q_ref, o_ref, lse_ref, normed):
    j = pl.program_id(0)

    @pl.when(j == 0)
    def _():
        normed[:TS, :] = normalize(own_ref[...], gain_ref[...])
        normed[TS:, :] = normalize(near_ref[...], gain_ref[...])
        lse_ref[...] = jnp.zeros_like(lse_ref)

    q = dot(normed[:TS, :], wq_ref[...]).astype(jnp.bfloat16)
    k = dot(normed[...], wk_ref[...]).astype(jnp.bfloat16)
    v = dot(normed[...], wv_ref[...]).astype(jnp.bfloat16)
    q_ref[...] = q
    bias = jnp.where(flag_ref[0] > 0, 0.0, OFF)
    lane = lax.broadcasted_iota(jnp.int32, lse_ref.shape, 1)
    for i in range(2):
        cut = slice(i * HD, (i + 1) * HD)
        s = dot_t(q[:, cut], k[:, cut])
        s0, s1 = s[:, :TS], s[:, TS:] + bias
        m = jnp.maximum(jnp.max(s0, axis=1, keepdims=True), jnp.max(s1, axis=1, keepdims=True)) * SCALE
        p0 = jnp.exp2(s0 * SCALE - m)
        p1 = jnp.exp2(s1 * SCALE - m)
        total = jnp.sum(p0, axis=1, keepdims=True) + jnp.sum(p1, axis=1, keepdims=True)
        o = dot(p0.astype(jnp.bfloat16), v[:TS, cut]) + dot(p1.astype(jnp.bfloat16), v[TS:, cut])
        o_ref[:, cut] = o / total
        lse_ref[...] = jnp.where(lane == 2 * j + i, m + jnp.log2(total), lse_ref[...])


def far_kernel(flag_ref, own_ref, far_ref, gain_ref, q_ref, o_ref, lse_ref, wk_ref, wv_ref, wo_hbm, out_ref, normed, mixed, wo, sem):
    j = pl.program_id(0)
    copy = pltpu.make_async_copy(wo_hbm, wo, sem)

    @pl.when(j == 0)
    def _():
        copy.start()
        normed[...] = normalize(far_ref[...], gain_ref[...])

    k = dot(normed[...], wk_ref[...]).astype(jnp.bfloat16)
    v = dot(normed[...], wv_ref[...]).astype(jnp.bfloat16)
    bias = jnp.where(flag_ref[0] > 0, 0.0, OFF)
    lane = lax.broadcasted_iota(jnp.int32, lse_ref.shape, 1)
    parts = []
    for i in range(2):
        cut = slice(i * HD, (i + 1) * HD)
        s = dot_t(q_ref[:, cut], k[:, cut]) + bias
        m = jnp.max(s, axis=1, keepdims=True) * SCALE
        p = jnp.exp2(s * SCALE - m)
        total = jnp.sum(p, axis=1, keepdims=True)
        o = dot(p.astype(jnp.bfloat16), v[:, cut])
        before = jnp.sum(jnp.where(lane == 2 * j + i, lse_ref[...], 0.0), axis=1, keepdims=True)
        top = jnp.maximum(before, m)
        w0 = jnp.exp2(before - top)
        w1 = jnp.exp2(m - top)
        r = 1.0 / (w0 + w1 * total)
        parts.append((o_ref[:, cut] * (w0 * r) + o * (w1 * r)).astype(jnp.bfloat16))
    mixed[j] = jnp.concatenate(parts, axis=1)

    @pl.when(j == PAIRS - 1)
    def _():
        copy.wait()
        row = jnp.concatenate([mixed[i] for i in range(PAIRS)], axis=1)
        out_ref[...] = (own_ref[...].astype(jnp.float32) + dot(row, wo[...])).astype(jnp.bfloat16)


def smem():
    return pl.BlockSpec(memory_space=pltpu.SMEM)


def whole(shape):
    return pl.BlockSpec(shape, lambda j: (0, 0))


def columns(rows, first):
    return pl.BlockSpec((rows, PAIR), lambda j: (0, first + j))


def near_attention(flag, own, near, gain, wqkv):
    return pl.pallas_call(
        near_kernel,
        grid=(PAIRS,),
        out_shape=(
            jax.ShapeDtypeStruct((TS, D), jnp.bfloat16),
            jax.ShapeDtypeStruct((TS, D), jnp.float32),
            jax.ShapeDtypeStruct((TS, HD), jnp.float32),
        ),
        in_specs=[
            smem(),
            whole((TS, D)),
            whole((TS, D)),
            whole((1, D)),
            columns(D, 0),
            columns(D, PAIRS),
            columns(D, 2 * PAIRS),
        ],
        out_specs=(columns(TS, 0), columns(TS, 0), whole((TS, HD))),
        scratch_shapes=[pltpu.VMEM((2 * TS, D), jnp.bfloat16)],
        compiler_params=pltpu.CompilerParams(vmem_limit_bytes=40 * 2**20),
        cost_estimate=pl.CostEstimate(flops=13 * 10**9, bytes_accessed=20 * 2**20, transcendentals=4 * 10**6),
        name="near_attention",
    )(flag, own, near, gain, wqkv, wqkv, wqkv)


def far_attention(flag, own, far, gain, q, o, lse, wqkv, wo):
    return pl.pallas_call(
        far_kernel,
        grid=(PAIRS,),
        out_shape=jax.ShapeDtypeStruct((TS, D), jnp.bfloat16),
        in_specs=[
            smem(),
            whole((TS, D)),
            whole((TS, D)),
            whole((1, D)),
            columns(TS, 0),
            columns(TS, 0),
            whole((TS, HD)),
            columns(D, PAIRS),
            columns(D, 2 * PAIRS),
            pl.BlockSpec(memory_space=pl.ANY),
        ],
        out_specs=whole((TS, D)),
        scratch_shapes=[
            pltpu.VMEM((TS, D), jnp.bfloat16),
            pltpu.VMEM((PAIRS, TS, PAIR), jnp.bfloat16),
            pltpu.VMEM((D, D), jnp.bfloat16),
            pltpu.SemaphoreType.DMA,
        ],
        compiler_params=pltpu.CompilerParams(vmem_limit_bytes=40 * 2**20),
        cost_estimate=pl.CostEstimate(flops=8 * 10**9, bytes_accessed=20 * 2**20, transcendentals=2 * 10**6),
        name="far_attention",
    )(flag, own, far, gain, q, o, lse, wqkv, wqkv, wo)


def place(t):
    z, r = divmod(t, 4)
    if r == 0:
        return 4 * ((z - 1) % 4) + 1
    if r == 3:
        return 4 * z
    return 4 * z + 1 + r


def other(t):
    return t + 1 if t % 2 else t - 1


def route(moves):
    return [(s * N_TILE + a, (s + step) % N_SECTION * N_TILE + b) for s in range(N_SECTION) for step, a, b in moves]


TILES = range(N_TILE)
CORE_SWAP = route([(0, t, t ^ 1) for t in TILES])
NEXT_CHIP = route([(0, t, other(t)) for t in TILES if 0 <= other(t) < N_TILE])
FORWARD = route([(1, t, place(t)) for t in TILES])
FORWARD_PAIR = route([(1, t, place(t ^ 1)) for t in TILES])
HOME = route([(1, place(t), t) for t in TILES])
SPREAD = [(t, place(t)) for t in TILES]


def on_device(latents, wqkv, wo, gains, lists, counts):
    own = latents[0]
    wqkv, wo = wqkv[0], wo[0]
    send = functools.partial(lax.ppermute, axis_name=BOTH)
    far = send(own, perm=NEXT_CHIP)
    near = send(own, perm=CORE_SWAP)
    tile = lax.axis_index("tile")
    pair = tile ^ 1
    beyond = jnp.where(tile % 2 == 1, tile + 1, tile - 1)
    used = jnp.arange(lists.shape[1]) < counts[0]
    pair_used = jnp.any((lists[0] == pair) & used).astype(jnp.int32)
    beyond_used = jnp.any((lists[0] == beyond) & used).astype(jnp.int32)
    flags = jnp.stack([pair_used, beyond_used])
    flags_next = lax.ppermute(flags, "tile", SPREAD)

    q, o, lse = near_attention(flags[:1], own, near, gains, wqkv)
    own = far_attention(flags[1:], own, far, gains, q, o, lse, wqkv, wo)
    far = send(own, perm=FORWARD_PAIR)
    own = send(own, perm=FORWARD)
    near = send(own, perm=CORE_SWAP)
    q, o, lse = near_attention(flags_next[1:], own, near, gains, wqkv)
    own = far_attention(flags_next[:1], own, far, gains, q, o, lse, wqkv, wo)
    return send(own, perm=HOME)[None]


def solution(mesh):
    return jax.shard_map(
        on_device,
        mesh=mesh,
        in_specs=(
            P("section", "tile", None),
            P("section", None, None),
            P("section", None, None),
            P("section", None),
            P("tile", None),
            P("tile"),
        ),
        out_specs=P("section", "tile", None),
        check_vma=False,
    )
```

time: 380 us -> 159 us (0.42)
  the two profiles are of different devices: /device:TPU:33 before, /device:TPU:97 now
where the time goes in v1:
time: 159 us
  Pallas kernels  71.3 us (45%)
  waiting for transfers between devices  66.9 us (42%)
  starting transfers between devices  13.7 us (9%)
  local copies, waits for them, and re-layouts  3.9 us (2%)
  between operations  1.99 us (1%)
    pallas_call x2, Pallas kernels, near_attention(): pl.pallas_call(near_kernel, grid=(PAIRS,), out_shape=(jax.ShapeDtypeStruc...  41.5 us
    ppermute x1, waiting for transfers between devices, on_device(): return send(own, perm=HOME)[None]  29.9 us
    pallas_call x2, Pallas kernels, far_attention(): pl.pallas_call(far_kernel, grid=(PAIRS,), out_shape=jax.ShapeDtypeStruct(...  29.7 us
    ppermute x1, waiting for transfers between devices, on_device(): own = send(own, perm=FORWARD)  25.6 us
    ppermute x1, waiting for transfers between devices, on_device(): far = send(own, perm=FORWARD_PAIR)  8.32 us
    ppermute x1, starting transfers between devices, on_device(): far = send(own, perm=NEXT_CHIP)  4.7 us
    ppermute x2, starting transfers between devices, on_device(): near = send(own, perm=CORE_SWAP)  4.51 us
    ppermute x1, starting transfers between devices, on_device(): own = send(own, perm=FORWARD)  3.35 us
  transfers between devices with their start and end apart: 7, of which 4 were waited for; matrix products, arithmetic and copies ran while one was open for 1% of the time, Pallas kernels for 26%

profile of v1, /device:TPU:97, one launch (start us, length us, event | category | flops | bytes accessed | tf_op | source)
XLA Modules:
  0.0 159.2 jit_solution(3939706527265479240)
XLA Ops:
  0.0 0.7 collective-permute-start.2
  0.7 4.7 %collective-permute-start.1 = (bf16[384,1536]{1,0:T(8,128)(2,1)}, bf16[384,1536]{1,0:T(8,128)(2,1)S(1)}, u32[]{:S(2)}, u32[]{:S(2)}) collective-permute-start(bf16[384,1536]{1,0:T(8,128)(2,1)} %bitcast.21), channel_id=1, source_target_pairs={{1,2},{2,1},{3,4},{4,3},{5,6},{6,5},{7,8},{8,7},{9,10},{10,9},{11,... | collective-permute-start | bytes 3538952 | tf_op jit(solution)/shard_map/ppermute | solution.py:200
  6.0 1.3 fusion.1
  8.6 0.0 collective-permute-done.2.near_ref
  8.6 0.0 slice-start
  8.6 0.0 copy-start
  8.6 1.4 copy-done
  10.0 0.9 copy-done.2
  10.9 20.5 %near_attention.2 = (bf16[384,1536]{1,0:T(8,128)(2,1)S(1)}, f32[384,1536]{1,0:T(8,128)S(1)}, f32[384,128]{1,0:T(8,128)S(1)}) custom-call(s32[1]{0:T(128)} %bitcast.2.flag_ref, bf16[384,1536]{1,0:T(8,128)(2,1)S(1)} %bitcast.22, bf16[384,1536]{1,0:T(8,128)(2,1)S(1)} %collective-permute-done.2.near_ref, f32[1,1536]{1,0:T(1,128)S(1)} %copy-done.2, ...), custom_call_target="tpu_custom_call" | custom-call | flops 12999999488 | bytes 20971520 | tf_op jit(solution)/shard_map/near_attention/pallas_call | solution.py:115
  31.4 14.6 %far_attention.2 = bf16[384,1536]{1,0:T(8,128)(2,1)S(1)} custom-call(s32[1]{0:T(128)} %bitcast.4.flag_ref, bf16[384,1536]{1,0:T(8,128)(2,1)S(1)} %bitcast.23, bf16[384,1536]{1,0:T(8,128)(2,1)S(1)} %collective-permute-done.1.far_ref, f32[1,1536]{1,0:T(1,128)S(1)} %copy-done.2, bf16[384,1536]{1,0:T(8,128)(2,1)S(1)} %get-tuple-element.11.q_ref, ...), custom_call_target="tpu_custom_call" | custom-call | flops 8000000000 | bytes 20971520 | tf_op jit(solution)/shard_map/far_attention/pallas_call | solution.py:141
  46.0 3.4 %collective-permute-start.3 = (bf16[384,1536]{1,0:T(8,128)(2,1)S(1)}, bf16[384,1536]{1,0:T(8,128)(2,1)S(1)}, u32[]{:S(2)}, u32[]{:S(2)}) collective-permute-start(bf16[384,1536]{1,0:T(8,128)(2,1)S(1)} %far_attention.2), channel_id=1, source_target_pairs={{0,29},{1,18},{2,19},{3,16},{4,17},{5,22},{6,23},{7,20},{8,21},{9,... | collective-permute-start | bytes 3538952 | tf_op jit(solution)/shard_map/ppermute | solution.py:214
  49.4 25.6 %collective-permute-done.3.own_ref = bf16[384,1536]{1,0:T(8,128)(2,1)S(1)} collective-permute-done((bf16[384,1536]{1,0:T(8,128)(2,1)S(1)}, bf16[384,1536]{1,0:T(8,128)(2,1)S(1)}, u32[]{:S(2)}, u32[]{:S(2)}) %collective-permute-start.3) | collective-permute-done | bytes 1179680 | tf_op jit(solution)/shard_map/ppermute | solution.py:214
  74.9 3.8 %collective-permute-start.5 = (bf16[384,1536]{1,0:T(8,128)(2,1)S(1)}, bf16[384,1536]{1,0:T(8,128)(2,1)S(1)}, u32[]{:S(2)}, u32[]{:S(2)}) collective-permute-start(bf16[384,1536]{1,0:T(8,128)(2,1)S(1)} %collective-permute-done.3.own_ref), channel_id=1, source_target_pairs={{0,1},{1,0},{2,3},{3,2},{4,5},{5,4},{6,7},{7,6},{8,9},{9,8},{10,11... | collective-permute-start | bytes 3538952 | tf_op jit(solution)/shard_map/ppermute | solution.py:215
  78.8 0.1 pad_add_fusion
  78.9 1.1 collective-permute-start
  79.9 3.1 %collective-permute-done = s32[2]{0:T(128)S(1)} collective-permute-done((s32[2]{0:T(128)S(1)}, s32[2]{0:T(128)S(1)}, u32[]{:S(2)}, u32[]{:S(2)}) %collective-permute-start) | collective-permute-done | bytes 40 | tf_op jit(solution)/shard_map/ppermute | solution.py:209
  83.0 0.6 fusion.2
  83.6 0.0 collective-permute-start.4
  83.6 21.0 %near_attention.3 = (bf16[384,1536]{1,0:T(8,128)(2,1)S(1)}, f32[384,1536]{1,0:T(8,128)S(1)}, f32[384,128]{1,0:T(8,128)S(1)}) custom-call(s32[1]{0:T(128)} %get-tuple-element.19.flag_ref, bf16[384,1536]{1,0:T(8,128)(2,1)S(1)} %collective-permute-done.3.own_ref, bf16[384,1536]{1,0:T(8,128)(2,1)S(1)} %collective-permute-done.5.near_ref, ...), custom_call_target="tpu_custom_call" | custom-call | flops 12999999488 | bytes 20971520 | tf_op jit(solution)/shard_map/near_attention/pallas_call | solution.py:115
  104.7 8.3 %collective-permute-done.4.far_ref = bf16[384,1536]{1,0:T(8,128)(2,1)S(1)} collective-permute-done((bf16[384,1536]{1,0:T(8,128)(2,1)S(1)}, bf16[384,1536]{1,0:T(8,128)(2,1)S(1)}, u32[]{:S(2)}, u32[]{:S(2)}) %collective-permute-start.4) | collective-permute-done | bytes 1179680 | tf_op jit(solution)/shard_map/ppermute | solution.py:213
  113.0 15.2 %far_attention.3 = bf16[384,1536]{1,0:T(8,128)(2,1)S(1)} custom-call(s32[1]{0:T(128)} %get-tuple-element.20.flag_ref, bf16[384,1536]{1,0:T(8,128)(2,1)S(1)} %collective-permute-done.3.own_ref, bf16[384,1536]{1,0:T(8,128)(2,1)S(1)} %collective-permute-done.4.far_ref, f32[1,1536]{1,0:T(1,128)S(1)} %copy-done.2, bf16[384,1536]{1,0:T(8,128)(2,1)S(1)} %get-tuple-element.14.q_ref, ...), custom_call_target="tpu_custom_call" | custom-call | flops 8000000000 | bytes 20971520 | tf_op jit(solution)/shard_map/far_attention/pallas_call | solution.py:141
  128.2 0.1 collective-permute-start.6
  128.2 29.9 %collective-permute-done.6 = bf16[384,1536]{1,0:T(8,128)(2,1)S(1)} collective-permute-done((bf16[384,1536]{1,0:T(8,128)(2,1)S(1)}, bf16[384,1536]{1,0:T(8,128)(2,1)S(1)}, u32[]{:S(2)}, u32[]{:S(2)}) %collective-permute-start.6) | collective-permute-done | bytes 1179680 | tf_op jit(solution)/shard_map/ppermute | solution.py:218
  158.1 1.0 copy.9
  (9 shorter events, 0.0 us)
Async XLA Ops:
  0.0 8.6 %collective-permute-start.2 = (bf16[384,1536]{1,0:T(8,128)(2,1)}, bf16[384,1536]{1,0:T(8,128)(2,1)S(1)}, u32[]{:S(2)}, u32[]{:S(2)}) collective-permute-start(bf16[384,1536]{1,0:T(8,128)(2,1)} %bitcast.20), channel_id=1, source_target_pairs={{0,1},{1,0},{2,3},{3,2},{4,5},{5,4},{6,7},{7,6},{8,9},{9,8},{10,11... | collective-permute-start | bytes 3538952 | tf_op jit(solution)/shard_map/ppermute | solution.py:201
  0.7 30.7 %collective-permute-start.1 = (bf16[384,1536]{1,0:T(8,128)(2,1)}, bf16[384,1536]{1,0:T(8,128)(2,1)S(1)}, u32[]{:S(2)}, u32[]{:S(2)}) collective-permute-start(bf16[384,1536]{1,0:T(8,128)(2,1)} %bitcast.21), channel_id=1, source_target_pairs={{1,2},{2,1},{3,4},{4,3},{5,6},{6,5},{7,8},{8,7},{9,10},{10,9},{11,... | collective-permute-start | bytes 3538952 | tf_op jit(solution)/shard_map/ppermute | solution.py:200
  8.6 22.8 %slice-start = ((s8[4718592]{0:T(1024)(128)(4,1)}), s8[4194304]{0:T(1024)(128)(4,1)S(1)}, s32[]{:S(2)}) async-start(s8[4718592]{0:T(1024)(128)(4,1)} %bitcast.16), calls=%async_computation | async-start | bytes 8388608
  8.6 1.4 copy-start
  10.0 0.9 copy-start.2
  10.9 20.5 %slice-start.1 = ((s8[4718592]{0:T(1024)(128)(4,1)}), s8[524288]{0:T(1024)(128)(4,1)S(1)}, s32[]{:S(2)}) async-start(s8[4718592]{0:T(1024)(128)(4,1)} %bitcast.16), calls=%async_computation.1 | async-start | bytes 1048576
  10.9 20.5 %copy-start.1 = (bf16[1,384,1536]{2,1,0:T(8,128)(2,1)S(1)}, bf16[1,384,1536]{2,1,0:T(8,128)(2,1)}, u32[]{:S(2)}) copy-start(bf16[1,384,1536]{2,1,0:T(8,128)(2,1)} %param.6) | copy-start | bytes 3538948
  46.0 28.9 %collective-permute-start.3 = (bf16[384,1536]{1,0:T(8,128)(2,1)S(1)}, bf16[384,1536]{1,0:T(8,128)(2,1)S(1)}, u32[]{:S(2)}, u32[]{:S(2)}) collective-permute-start(bf16[384,1536]{1,0:T(8,128)(2,1)S(1)} %far_attention.2), channel_id=1, source_target_pairs={{0,29},{1,18},{2,19},{3,16},{4,17},{5,22},{6,23},{7,20},{8,21},{9,... | collective-permute-start | bytes 3538952 | tf_op jit(solution)/shard_map/ppermute | solution.py:214
  74.9 8.7 %collective-permute-start.5 = (bf16[384,1536]{1,0:T(8,128)(2,1)S(1)}, bf16[384,1536]{1,0:T(8,128)(2,1)S(1)}, u32[]{:S(2)}, u32[]{:S(2)}) collective-permute-start(bf16[384,1536]{1,0:T(8,128)(2,1)S(1)} %collective-permute-done.3.own_ref), channel_id=1, source_target_pairs={{0,1},{1,0},{2,3},{3,2},{4,5},{5,4},{6,7},{7,6},{8,9},{9,8},{10,11... | collective-permute-start | bytes 3538952 | tf_op jit(solution)/shard_map/ppermute | solution.py:215
  78.9 4.2 %collective-permute-start = (s32[2]{0:T(128)S(1)}, s32[2]{0:T(128)S(1)}, u32[]{:S(2)}, u32[]{:S(2)}) collective-permute-start(s32[2]{0:T(128)S(1)} %pad_add_fusion), channel_id=1, source_target_pairs={{0,13},{1,2},{2,3},{3,0},{4,1},{5,6},{6,7},{7,4},{8,5},{9,10},{10,... | collective-permute-start | bytes 32 | tf_op jit(solution)/shard_map/ppermute | solution.py:209
  83.6 29.4 %collective-permute-start.4 = (bf16[384,1536]{1,0:T(8,128)(2,1)S(1)}, bf16[384,1536]{1,0:T(8,128)(2,1)S(1)}, u32[]{:S(2)}, u32[]{:S(2)}) collective-permute-start(bf16[384,1536]{1,0:T(8,128)(2,1)S(1)} %far_attention.2), channel_id=1, source_target_pairs={{0,18},{1,29},{2,16},{3,19},{4,22},{5,17},{6,20},{7,23},{8,26},{9,... | collective-permute-start | bytes 3538952 | tf_op jit(solution)/shard_map/ppermute | solution.py:213
  128.2 30.0 %collective-permute-start.6 = (bf16[384,1536]{1,0:T(8,128)(2,1)S(1)}, bf16[384,1536]{1,0:T(8,128)(2,1)S(1)}, u32[]{:S(2)}, u32[]{:S(2)}) collective-permute-start(bf16[384,1536]{1,0:T(8,128)(2,1)S(1)} %far_attention.3), channel_id=1, source_target_pairs={{13,16},{2,17},{3,18},{0,19},{1,20},{6,21},{7,22},{4,23},{5,24},{1... | collective-permute-start | bytes 3538952 | tf_op jit(solution)/shard_map/ppermute | solution.py:218
